TPU v7x, 32 devices: a whole 2x2x4 slice. The times are simulated.
32 devices in a mesh: col: 8 (over z, y), row: 4 (over x, core).
Axes of the slice: x: 2, y: 2, z: 4, core: 2. Of those that a mesh axis runs over, the one named last changes fastest.
Arguments:
- panel: int32 [8], replicated, may hold values from 0 to 7, each once
- centres_cols: bfloat16 [4096, 1024], P('col'), may hold values from -1 to 1
- centres_rows: bfloat16 [128, 1024], P(('row', 'col')), may hold values from -1 to 1
- diag_inverse: float32 [4096, 512], P('col'), as said below
- trailing: float32 [128, 4096], P('row', 'col'), may hold values from -6 to 6
Outputs:
- updated: float32 [128, 4096], P('row', 'col')
Inputs may be any that keep to these rules, and one draw needn't show every extreme that they name: panel holds each of 0 to 7 once. Each 512 x 512 block of diag_inverse is lower triangular with a positive diagonal.
All inputs are finite; a program needn't handle non-finite values.
Results may differ from a plain program's by a relative error of at most 0.0003.
Values may be sent and summed in bfloat16 or wider, within the bound.
A program may use at most 64 MiB of HBM per device.

v0:
```python
import math

import jax
import jax.numpy as jnp
from jax import lax
from jax.sharding import PartitionSpec as P

LAYERS = 3


def broadcast(shard, axis, root):
    mine = lax.axis_index(axis) == root
    return lax.psum(jnp.where(mine, shard, jnp.zeros_like(shard)), axis)


def kernel(left, right):
    gram = lax.dot_general(
        left, right, (((1,), (1,)), ((), ())), preferred_element_type=jnp.float32
    )
    left_f = left.astype(jnp.float32)
    right_f = right.astype(jnp.float32)
    inv_left = 1.0 / jnp.sqrt(jnp.sum(left_f * left_f, axis=1) + 1e-06)
    inv_right = 1.0 / jnp.sqrt(jnp.sum(right_f * right_f, axis=1) + 1e-06)
    cosine = gram * inv_left[:, None] * inv_right[None, :]
    theta = cosine
    rho_now = cosine
    for layer in range(LAYERS):
        angle_now = jnp.arccos(rho_now)
        zero_order = (math.pi - angle_now) / math.pi
        rho_next = (jnp.sqrt(1.0 - rho_now * rho_now) + (math.pi - angle_now) * rho_now) / math.pi
        theta = theta * zero_order + rho_next
        rho_now = rho_next
    return theta / (inv_left[:, None] * inv_right[None, :])


def apply_inverse(values, inverse):
    return lax.dot_general(
        values,
        inverse,
        (((1,), (1,)), ((), ())),
        precision=lax.Precision.HIGHEST,
        preferred_element_type=jnp.float32,
    )


def on_device(panel, centres_cols, centres_rows, diag_inverse, trailing):
    col_count = lax.axis_size("col")
    target_rank = col_count // 4
    block_ids = jnp.arange(col_count, dtype=jnp.int32)
    panel_at = jnp.sum(jnp.where(panel == target_rank, block_ids, 0))
    panel_x = broadcast(centres_cols, "col", panel_at)
    panel_inv = broadcast(diag_inverse, "col", panel_at)

    def panel_rows_of(piece):
        return apply_inverse(kernel(piece, panel_x), panel_inv)

    rows_l = panel_rows_of(lax.all_gather(centres_rows, "col", axis=0, tiled=True))
    cols_l = panel_rows_of(centres_cols)
    update = lax.dot_general(
        rows_l,
        cols_l,
        (((1,), (1,)), ((), ())),
        precision=lax.Precision.HIGHEST,
        preferred_element_type=jnp.float32,
    )
    block_here = lax.axis_index("col")
    own_rank = lax.dynamic_index_in_dim(panel, block_here, 0, keepdims=False)
    return jnp.where(own_rank > target_rank, trailing - update, trailing)


def solution(mesh):
    return jax.shard_map(
        on_device,
        mesh=mesh,
        in_specs=(P(), P("col", None), P(("row", "col"), None), P("col", None), P("row", "col")),
        out_specs=P("row", "col"),
        check_vma=False,
    )
```

profile of v0, /device:TPU:1, one launch (start us, length us, event | category | flops | bytes accessed | tf_op | source)
XLA Modules:
  0.0 194.8 jit_solution(7392399040223993213)
XLA Ops:
  6.5 0.0 all-reduce.3.cloned.1.call-start
  6.5 1.3 fusion.111
  8.5 1.1 broadcast_select_fusion
  9.5 0.0 copy-start.2
  9.5 0.0 all-reduce.3.cloned.1.call-update
  9.6 0.0 all-reduce.5.cloned.1.call-start
  9.6 1.1 copy-done.2
  10.8 1.1 broadcast_select_fusion.1
  11.8 0.0 copy-start
  11.8 0.0 copy-start.5
  11.8 0.0 copy-start.6
  11.9 0.0 all-reduce.5.cloned.1.call-update
  11.9 1.2 copy-done
  13.1 0.3 multiply_reduce_fusion
  13.4 0.0 copy-done.5
  13.4 27.0 %all-gather = bf16[8,4,1024]{2,1,0:T(4,128)(2,1)S(1)} all-gather(bf16[1,4,1024]{2,1,0:T(4,128)(2,1)S(1)} %bitcast.14), channel_id=1, replica_groups=mesh['col'=8,'row'=4] {'col'}, dimensions={0}, use_global_device_ids=true | all-gather | bytes 73728 | tf_op jit(solution)/shard_map/all_gather | solution.py:57
  40.4 0.1 multiply_reduce_fusion.2
  40.5 0.0 copy-done.6
  40.5 0.6 dynamic_slice.4
  41.7 48.7 %all-reduce.3.cloned.1.call-done = bf16[512,1024]{1,0:T(8,128)(2,1)} async-done(((bf16[512,1024]{1,0:T(8,128)(2,1)}), bf16[512,1024]{1,0:T(8,128)(2,1)}) %all-reduce.3.cloned.1.call-update) | async-done | bytes 1048592 | tf_op jit(solution)/shard_map/psum | solution.py:13
  90.5 1.6 multiply_reduce_fusion.1
  92.1 0.0 copy-done.1
  92.1 0.4 fusion.4
  92.5 0.7 fusion.1
  93.3 78.7 %all-reduce.5.cloned.1.call-done = f32[512,512]{1,0:T(8,128)} async-done(((f32[512,512]{1,0:T(8,128)}), f32[512,512]{1,0:T(8,128)}) %all-reduce.5.cloned.1.call-update) | async-done | bytes 1048592 | tf_op jit(solution)/shard_map/psum | solution.py:13
  172.0 0.0 copy-start.3
  172.0 2.8 %fusion.58 = f32[32,512]{1,0:T(8,128)S(1)} fusion(f32[512,512]{1,0:T(8,128)} %all-reduce.5.cloned.1.call-done, f32[32,512]{1,0:T(8,128)S(1)} %fusion.4, f32[512]{0:T(512)S(1)} %add_rsqrt_fusion.1, f32[32]{0:T(128)S(1)} %add_rsqrt_fusion.2), kind=kOutput, calls=%fused_computation.66 | convolution fusion | flops 101285888 | bytes 1181824 | tf_op jit(solution)/shard_map/dot_general | solution.py:37
  174.8 0.0 copy-done.3
  174.8 0.0 copy-start.4
  174.8 11.5 %fusion.5 = f32[512,512]{1,0:T(8,128)S(1)} fusion(f32[512,512]{1,0:T(8,128)S(1)} %copy-done.3, f32[512,512]{0,1:T(8,128)S(1)} %fusion.1, f32[512]{0:T(512)S(1)} %add_rsqrt_fusion.1, f32[512]{0:T(512)S(1)} %add_rsqrt_fusion), kind=kOutput, calls=%fused_computation.10 | convolution fusion | flops 1620574208 | bytes 3149824 | tf_op jit(solution)/shard_map/dot_general | solution.py:37
  186.3 0.0 copy-done.4
  186.3 1.7 fusion.2
  (5 shorter events, 0.0 us)
Async XLA Ops:
  6.5 83.9 %all-reduce.3.cloned.1.call-start = ((), (), s32[]{:S(2)}) async-start(), calls=%async_computation | async-start | bytes 2097152 | tf_op jit(solution)/shard_map/psum | solution.py:13
  9.5 1.2 copy-start.2
  9.6 162.4 %all-reduce.5.cloned.1.call-start = ((), (), s32[]{:S(2)}) async-start(), calls=%async_computation.1 | async-start | bytes 2097152 | tf_op jit(solution)/shard_map/psum | solution.py:13
  11.8 1.2 copy-start
  11.8 1.5 copy-start.5
  11.8 28.6 %copy-start.6 = (s32[8]{0:T(128)S(1)}, s32[8]{0:T(128)}, u32[]{:S(2)}) copy-start(s32[8]{0:T(128)} %param.5) | copy-start | bytes 100
  90.5 1.6 copy-start.1
  172.0 2.8 %copy-start.3 = (f32[512,512]{1,0:T(8,128)S(1)}, f32[512,512]{1,0:T(8,128)}, u32[]{:S(2)}) copy-start(f32[512,512]{1,0:T(8,128)} %all-reduce.5.cloned.1.call-done) | copy-start | bytes 3145732
  174.8 11.5 %copy-start.4 = (f32[32,512]{1,0:T(8,128)S(1)}, f32[32,512]{1,0:T(8,128)}, u32[]{:S(2)}) copy-start(f32[32,512]{1,0:T(8,128)} %param.9) | copy-start | bytes 196612
Sparse Core Ops, SparseCore 0:
  10.9 79.5 all-reduce.2
  94.4 77.5 all-reduce.4
where the time goes:
time: 196 us; the launch traced here: 195 us
  waiting for transfers between devices  128 us (65%)
  blocking collectives  27 us (14%)
  matrix products  17.1 us (9%)
  between operations  14.8 us (8%)
  other arithmetic  5.44 us (3%)
  local copies, waits for them, and re-layouts  2.98 us (2%)
    psum x2, waiting for transfers between devices, broadcast(): return lax.psum(jnp.where(mine, shard, jnp.zeros_like(shard)), axis)  127 us
    all_gather x1, blocking collectives, on_device(): lax.all_gather(centres_rows, 'col', axis=0, tiled=True)  27 us
    dot_general x2, matrix products, apply_inverse(): lax.dot_general(values, inverse, (((1,), (1,)), ((), ())), precision=lax....  14.3 us
  transfers between devices with their start and end apart: 2, of which 2 were waited for; matrix products, arithmetic and copies ran while one was open for 2% of the time, Pallas kernels for 0%

commit v1 on v0

v1 whole, which is shorter than its diff:
```python
import functools
import math

import jax
import jax.numpy as jnp
from jax import lax
from jax.experimental import pallas as pl
from jax.experimental.pallas import tpu as pltpu
from jax.sharding import PartitionSpec as P

LAYERS = 3
EPS = 1e-06
CHUNKS = 4
MESH = pl.DeviceIdType.MESH
F32 = jnp.float32
BF16 = jnp.bfloat16
ACOS = tuple(
    v / math.pi
    for v in (
        1.5707963050, -0.2145988016, 0.0889789874, -0.0501743046,
        0.0308918810, -0.0170881256, 0.0066700901, -0.0012624911,
    )
)


def root(y):
    y = jnp.maximum(y, 1e-30)
    return y * lax.rsqrt(y)


def theta_of(u):
    rho = jnp.clip(u, -1.0, 1.0)
    theta = rho
    for layer in range(LAYERS):
        size = jnp.abs(rho) if layer == 0 else rho
        poly = jnp.full_like(size, ACOS[-1])
        for coef in ACOS[-2::-1]:
            poly = poly * size + coef
        low = root(1.0 - size)
        angle = low * poly
        sine = low * root(1.0 + size)
        if layer == 0:
            zero_order = jnp.where(rho < 0.0, angle, 1.0 - angle)
        else:
            zero_order = 1.0 - angle
        rho_next = sine * (1.0 / math.pi) + zero_order * rho
        theta = theta * zero_order + rho_next
        rho = rho_next
    return theta


def dot_t(a, b, precision=None):
    return lax.dot_general(
        a, b, (((1,), (1,)), ((), ())), precision=precision, preferred_element_type=F32
    )


def kernel(
    n, nr, panel, x_ref, rows_ref, inv_ref, trail_ref, out_ref,
    rows_buf, rows_all, py, pr, plft, w_out, wy, wr, wl, kt, part, part_in,
    rows_send, rows_recv, py_send, py_recv, pz_send, pz_recv,
    wx_send, wx_recv, wy_send, wy_recv, wz_send, wz_recv, pt_send, pt_recv,
):
    col = lax.axis_index("col")
    row = lax.axis_index("row")
    nz = n // 2
    z, y = col // 2, col % 2
    y_mate = z * 2 + 1 - y
    right, left = lax.rem(col + 2, n), lax.rem(col + n - 2, n)
    blk = x_ref.shape[0]
    quarter = blk // nr
    size = quarter // CHUNKS
    per = rows_ref.shape[0]
    group = per * n

    target = n // 4
    at = jnp.int32(0)
    for i in range(n):
        at = at + jnp.where(panel[i] == target, i, 0)
    root_here = at == col
    root_layer = at // 2 == z
    from_left = at // 2 <= z

    barrier = pltpu.get_barrier_semaphore()
    for d in range(1, n):
        pl.semaphore_signal(
            barrier, inc=1, device_id={"col": lax.rem(col + d, n)}, device_id_type=MESH
        )
    for d in range(1, nr):
        pl.semaphore_signal(
            barrier, inc=1, device_id={"row": lax.rem(row + d, nr)}, device_id_type=MESH
        )
    rows_buf[col] = rows_ref[...].astype(F32)
    pl.semaphore_wait(barrier, n - 1 + nr - 1)

    def remote(src, dst, send, recv, **where):
        return pltpu.make_async_remote_copy(
            src_ref=src, dst_ref=dst, send_sem=send, recv_sem=recv,
            device_id=where, device_id_type=MESH,
        )

    def rows_copy(d, slot):
        return remote(
            rows_buf.at[slot], rows_buf.at[slot], rows_send.at[d], rows_recv.at[slot],
            col=lax.rem(col + d, n),
        )

    for d in range(1, n):
        rows_copy(d, col).start()

    def own_chunk(k):
        return pl.ds(pl.multiple_of(row * quarter + k * size, size), size)

    def py_copy(k):
        return remote(x_ref.at[own_chunk(k)], py.at[k], py_send.at[k], py_recv.at[k], col=y_mate)

    for k in range(CHUNKS):
        py_copy(k).start()

    xf = x_ref[...].astype(F32)
    sq = xf * xf
    sq_hi = sq.astype(BF16)
    sq_lo = (sq - sq_hi.astype(F32)).astype(BF16)
    ones = jnp.ones((16, x_ref.shape[1]), BF16)
    x_sum = (dot_t(ones, sq_hi) + dot_t(ones, sq_lo))[0:1, :] + EPS
    x_norm = jnp.sqrt(x_sum)
    x_inv = 1.0 / x_norm

    def block_kernel(a, a_f):
        a_norm = jnp.sqrt(jnp.sum(a_f * a_f, axis=1, keepdims=True) + EPS)
        u = dot_t(a, x_ref[...]) * (1.0 / a_norm) * x_inv
        return theta_of(u) * (a_norm * x_norm)

    def z_copy(buf, k, way, send, recv):
        return remote(
            buf.at[k], buf.at[k], send.at[way, k], recv.at[way, k],
            col=right if way == 0 else left,
        )

    def flood(step, units, cand, bufs, send, recv):
        for way in (0, 1):
            pos = z if way == 0 else nz - 1 - z
            k = step - pos
            buf = bufs[way]

            @pl.when(jnp.logical_and(k >= 0, k < units))
            def _():
                @pl.when(pos == 0)
                def _():
                    buf[k] = cand(k)

                @pl.when(pos > 0)
                def _():
                    z_copy(buf, k, way, send, recv).wait_recv()
                    buf[k] = lax.select(root_layer, cand(k), buf[k])

                @pl.when(pos < nz - 1)
                def _():
                    z_copy(buf, k, way, send, recv).start()

    def flood_end(units, bufs, send, recv):
        for way in (0, 1):
            pos = z if way == 0 else nz - 1 - z

            @pl.when(pos < nz - 1)
            def _():
                for k in range(units):
                    z_copy(bufs[way], k, way, send, recv).wait_send()

    def panel_cand(k):
        return py[k]

    def panel_step(step):
        if step < CHUNKS:
            py_copy(step).wait_recv()
            own = x_ref[own_chunk(step), :]
            py[step] = lax.select(root_here, own, py[step])
        flood(step, CHUNKS, panel_cand, (pr, plft), pz_send, pz_recv)
        k = step - (nz - 1)
        if k >= 0:
            chunk = lax.select(from_left, pr[k], plft[k])
            kt[k * size:(k + 1) * size, :] = block_kernel(chunk, chunk.astype(F32))

    def work_rows():
        for d in range(1, n):
            slot = lax.rem(col + n - d, n)
            rows_copy(d, slot).wait_recv()
        for c in range(n):
            rows_all[c * per:(c + 1) * per, :] = rows_buf[c]
        a_f = rows_all[...]
        return block_kernel(a_f.astype(BF16), a_f)

    def wx_copy(d, slot):
        return remote(
            w_out.at[lax.rem(row + d, nr)], wy.at[nr + slot], wx_send.at[d], wx_recv.at[slot],
            row=lax.rem(row + d, nr),
        )

    def wy_copy(k):
        return remote(wy.at[nr + k], wy.at[k], wy_send.at[k], wy_recv.at[k], col=y_mate)

    def work_w(mid):
        w = jnp.dot(mid, inv_ref[...], precision=lax.Precision.HIGHEST, preferred_element_type=F32)
        for j in range(nr):
            w_out[j] = w[:, j * quarter:(j + 1) * quarter]
        for d in range(1, nr):
            wx_copy(d, row).start()
        wy[nr + row] = w_out[row]

    def work_exchange():
        for d in range(1, nr):
            wx_copy(d, lax.rem(row + nr - d, nr)).wait_recv()
        for k in range(nr):
            wy_copy(k).start()

    def w_step(step):
        if step < nr:
            wy_copy(step).wait_recv()
            wy[step] = lax.select(root_here, wy[nr + step], wy[step])
        flood(step, nr, lambda k: wy[k], (wr, wl), wz_send, wz_recv)

    panel_steps = CHUNKS + nz - 1
    w_steps = nr + nz - 1
    todo = list(range(panel_steps))
    k_rows = work_rows()
    panel_step(todo.pop(0))
    mid = dot_t(k_rows, inv_ref[...], lax.Precision.HIGHEST)
    panel_step(todo.pop(0))
    work_w(mid)
    panel_step(todo.pop(0))
    panel_step(todo.pop(0))
    work_exchange()
    for step in range(w_steps):
        if todo:
            panel_step(todo.pop(0))
        w_step(step)
    while todo:
        panel_step(todo.pop(0))

    def part_copy(d, slot):
        return remote(
            part.at[lax.rem(row + d, nr)], part_in.at[slot], pt_send.at[d], pt_recv.at[slot],
            row=lax.rem(row + d, nr),
        )

    for j in range(nr):
        w = lax.select(from_left, wr[j], wl[j])
        part[j] = jnp.dot(w, kt[...], precision=lax.Precision.HIGHEST, preferred_element_type=F32)
    for d in range(1, nr):
        part_copy(d, row).start()
    total = part[row]
    for d in range(1, nr):
        slot = lax.rem(row + nr - d, nr)
        part_copy(d, slot).wait_recv()
        total = total + part_in[slot]
    trail = trail_ref[...]
    out_ref[...] = lax.select(panel[col] > target, trail - total, trail)

    for d in range(1, n):
        rows_copy(d, col).wait_send()
    for k in range(CHUNKS):
        py_copy(k).wait_send()
    for d in range(1, nr):
        wx_copy(d, row).wait_send()
        part_copy(d, row).wait_send()
    for k in range(nr):
        wy_copy(k).wait_send()
    flood_end(CHUNKS, (pr, plft), pz_send, pz_recv)
    flood_end(nr, (wr, wl), wz_send, wz_recv)


def on_device(n, nr, panel, centres_cols, centres_rows, diag_inverse, trailing):
    blk, width = centres_cols.shape
    quarter = blk // nr
    size = quarter // CHUNKS
    per = centres_rows.shape[0]
    group = per * n
    dma = pltpu.SemaphoreType.DMA
    vmem = pl.BlockSpec(memory_space=pltpu.VMEM)
    return pl.pallas_call(
        functools.partial(kernel, n, nr),
        out_shape=jax.ShapeDtypeStruct(trailing.shape, F32),
        in_specs=[pl.BlockSpec(memory_space=pltpu.SMEM)] + [vmem] * 4,
        out_specs=vmem,
        scratch_shapes=[
            pltpu.VMEM((n, per, width), F32),
            pltpu.VMEM((group, width), F32),
            pltpu.VMEM((CHUNKS, size, width), BF16),
            pltpu.VMEM((CHUNKS, size, width), BF16),
            pltpu.VMEM((CHUNKS, size, width), BF16),
            pltpu.VMEM((nr, group, quarter), F32),
            pltpu.VMEM((2 * nr, group, quarter), F32),
            pltpu.VMEM((nr, group, quarter), F32),
            pltpu.VMEM((nr, group, quarter), F32),
            pltpu.VMEM((quarter, blk), F32),
            pltpu.VMEM((nr, group, blk), F32),
            pltpu.VMEM((nr, group, blk), F32),
            dma((n,)), dma((n,)),
            dma((CHUNKS,)), dma((CHUNKS,)),
            dma((2, CHUNKS)), dma((2, CHUNKS)),
            dma((nr,)), dma((nr,)),
            dma((nr,)), dma((nr,)),
            dma((2, nr)), dma((2, nr)),
            dma((nr,)), dma((nr,)),
        ],
        compiler_params=pltpu.CompilerParams(
            collective_id=0, has_side_effects=True, vmem_limit_bytes=48 * 2**20
        ),
    )(panel, centres_cols, centres_rows, diag_inverse, trailing)


def solution(mesh):
    return jax.shard_map(
        functools.partial(on_device, mesh.shape["col"], mesh.shape["row"]),
        mesh=mesh,
        in_specs=(P(), P("col", None), P(("row", "col"), None), P("col", None), P("row", "col")),
        out_specs=P("row", "col"),
        check_vma=False,
    )
```

time: 196 us -> 54 us (0.28)
  waiting for transfers between devices: 128 us -> 0 us
  Pallas kernels: 0 us -> 48.5 us
  blocking collectives: 27 us -> 0 us
  matrix products: 17.1 us -> 0 us
  between operations: 14.8 us -> 0.01 us
  other arithmetic: 5.44 us -> 0 us
  local copies, waits for them, and re-layouts: 2.98 us -> 5.27 us
    psum x2 -> x0, waiting for transfers between devices: 127 us -> none  [broadcast(): return lax.psum(jnp.where(mine, shard, jnp.zeros_like(shard)), axis)]
    pallas_call x0 -> x1, Pallas kernels: none -> 48.5 us  [on_device(): pl.pallas_call(functools.partial(kernel, n, nr), out_shape=jax.ShapeDtype...]
    all_gather x1 -> x0, blocking collectives: 27 us -> none  [on_device(): lax.all_gather(centres_rows, 'col', axis=0, tiled=True)]
    dot_general x5 -> x0, matrix products: 17.1 us -> none  [the longest x2 14.3 us: apply_inverse(): lax.dot_general(values, inverse, (((1,), (1,)), ((), ())), precision=lax....]
    reduce_sum x4 -> x0, other arithmetic: 3.28 us -> none  [the longest x1 1.59 us: kernel(): inv_right = 1.0 / jnp.sqrt(jnp.sum(right_f * right_f, axis=1) + 1e-06)]
    unnamed x15 -> x11, local copies, waits for them, and re-layouts: 2.39 us -> 5.27 us
    select_n x2 -> x0, other arithmetic: 2.14 us -> none  [broadcast(): return lax.psum(jnp.where(mine, shard, jnp.zeros_like(shard)), axis)]
  transfers between devices with their start and end apart: 2 -> 0, of which waited for: 2 -> 0; matrix products, arithmetic and copies ran while one was open for 2% -> 0% of each run, Pallas kernels for 0% -> 0%
where the time goes in v1:
time: 54 us; the launch traced here: 53.8 us
  Pallas kernels  48.5 us (90%)
  local copies, waits for them, and re-layouts  5.27 us (10%)
    pallas_call x1, Pallas kernels, on_device(): pl.pallas_call(functools.partial(kernel, n, nr), out_shape=jax.ShapeDtype...  48.5 us
    unnamed x11, local copies, waits for them, and re-layouts  5.27 us

profile of v1, /device:TPU:1, one launch (start us, length us, event | category | flops | bytes accessed | tf_op | source)
XLA Modules:
  0.0 53.8 jit_solution(1914658793149206268)
XLA Ops:
  0.0 0.0 copy-start
  0.0 1.2 %copy-done = bf16[512,1024]{1,0:T(8,128)(2,1)S(1)} copy-done((bf16[512,1024]{1,0:T(8,128)(2,1)S(1)}, bf16[512,1024]{1,0:T(8,128)(2,1)}, u32[]{:S(2)}) %copy-start) | copy-done | bytes 1048600
  1.2 0.0 copy-start.1
  1.2 1.2 %copy-done.1 = f32[512,512]{1,0:T(8,128)S(1)} copy-done((f32[512,512]{1,0:T(8,128)S(1)}, f32[512,512]{1,0:T(8,128)}, u32[]{:S(2)}) %copy-start.1) | copy-done | bytes 1048600
  2.5 0.0 copy-start.2
  2.5 0.8 %copy-done.2 = f32[32,512]{1,0:T(8,128)S(1)} copy-done((f32[32,512]{1,0:T(8,128)S(1)}, f32[32,512]{1,0:T(8,128)}, u32[]{:S(2)}) %copy-start.2) | copy-done | bytes 65560
  3.3 0.0 copy-start.3
  3.3 0.7 %copy-done.3 = bf16[4,1024]{1,0:T(4,128)(2,1)S(1)} copy-done((bf16[4,1024]{1,0:T(4,128)(2,1)S(1)}, bf16[4,1024]{1,0:T(4,128)(2,1)}, u32[]{:S(2)}) %copy-start.3) | copy-done | bytes 8216
  4.0 0.0 copy-start.4
  4.0 0.7 %copy-done.4 = s32[8]{0:T(128)S(1)} copy-done((s32[8]{0:T(128)S(1)}, s32[8]{0:T(128)}, u32[]{:S(2)}) %copy-start.4) | copy-done | bytes 56
  4.6 48.5 %shard_map.55 = f32[32,512]{1,0:T(8,128)S(1)} custom-call(s32[8]{0:T(128)S(1)} %copy-done.4, bf16[512,1024]{1,0:T(8,128)(2,1)S(1)} %copy-done, bf16[4,1024]{1,0:T(4,128)(2,1)S(1)} %copy-done.3, f32[512,512]{1,0:T(8,128)S(1)} %copy-done.1, f32[32,512]{1,0:T(8,128)S(1)} %copy-done.2), custom_call_target="tpu_custom_call" | custom-call | tf_op jit(solution)/shard_map/pallas_call | solution.py:280
  53.1 0.6 %copy.7 = f32[32,512]{1,0:T(8,128)} copy(f32[32,512]{1,0:T(8,128)S(1)} %shard_map.55) | data formatting | bytes 131072
Async XLA Ops:
  0.0 1.2 %copy-start = (bf16[512,1024]{1,0:T(8,128)(2,1)S(1)}, bf16[512,1024]{1,0:T(8,128)(2,1)}, u32[]{:S(2)}) copy-start(bf16[512,1024]{1,0:T(8,128)(2,1)} %x_ref.1) | copy-start | bytes 3145732
  1.2 1.2 %copy-start.1 = (f32[512,512]{1,0:T(8,128)S(1)}, f32[512,512]{1,0:T(8,128)}, u32[]{:S(2)}) copy-start(f32[512,512]{1,0:T(8,128)} %inv_ref.1) | copy-start | bytes 3145732
  2.5 0.8 %copy-start.2 = (f32[32,512]{1,0:T(8,128)S(1)}, f32[32,512]{1,0:T(8,128)}, u32[]{:S(2)}) copy-start(f32[32,512]{1,0:T(8,128)} %trail_ref.1) | copy-start | bytes 196612
  3.3 0.7 %copy-start.3 = (bf16[4,1024]{1,0:T(4,128)(2,1)S(1)}, bf16[4,1024]{1,0:T(4,128)(2,1)}, u32[]{:S(2)}) copy-start(bf16[4,1024]{1,0:T(4,128)(2,1)} %rows_ref.1) | copy-start | bytes 24580
  4.0 0.7 %copy-start.4 = (s32[8]{0:T(128)S(1)}, s32[8]{0:T(128)}, u32[]{:S(2)}) copy-start(s32[8]{0:T(128)} %panel.1) | copy-start | bytes 100

commit v2 on v1

v2 whole, which is shorter than its diff:
```python
import functools
import math

import jax
import jax.numpy as jnp
from jax import lax
from jax.experimental import pallas as pl
from jax.experimental.pallas import tpu as pltpu
from jax.sharding import PartitionSpec as P

LAYERS = 3
EPS = 1e-06
UNITS = 8
GROUPS = 2
HOP = 2
MESH = pl.DeviceIdType.MESH
F32 = jnp.float32
BF16 = jnp.bfloat16
ACOS = tuple(
    v / math.pi
    for v in (
        1.5707963050, -0.2145988016, 0.0889789874, -0.0501743046,
        0.0308918810, -0.0170881256, 0.0066700901, -0.0012624911,
    )
)


def root(y):
    y = jnp.maximum(y, 1e-30)
    return y * lax.rsqrt(y)


def theta_of(u):
    rho = jnp.clip(u, -1.0, 1.0)
    theta = rho
    for layer in range(LAYERS):
        size = jnp.abs(rho) if layer == 0 else rho
        poly = jnp.full_like(size, ACOS[-1])
        for coef in ACOS[-2::-1]:
            poly = poly * size + coef
        low = root(1.0 - size)
        angle = low * poly
        sine = low * root(1.0 + size)
        if layer == 0:
            zero_order = jnp.where(rho < 0.0, angle, 1.0 - angle)
        else:
            zero_order = 1.0 - angle
        rho_next = sine * (1.0 / math.pi) + zero_order * rho
        theta = theta * zero_order + rho_next
        rho = rho_next
    return theta


def dot_t(a, b, precision=None):
    return lax.dot_general(
        a, b, (((1,), (1,)), ((), ())), precision=precision, preferred_element_type=F32
    )


def split3(a):
    hi = a.astype(BF16)
    rest = a - hi.astype(F32)
    mid = rest.astype(BF16)
    return hi, mid, (rest - mid.astype(F32)).astype(BF16)


def product3(a, weights, transposed):
    m = a.shape[0]
    terms = jnp.concatenate(split3(a), axis=0)
    dims = (((1,), (1 if transposed else 0,)), ((), ()))

    def mul(count, w):
        return lax.dot_general(terms[:count * m], w, dims, preferred_element_type=F32)

    p, q, t = mul(3, weights[0]), mul(2, weights[1]), mul(1, weights[2])
    small = t + q[m:] + p[2 * m:]
    return (small + (q[:m] + p[m:2 * m])) + p[:m]


def kernel(
    n, nr, panel_hbm, x_hbm, rows_ref, inv_hbm, trail_hbm, out_ref,
    panel, x_ref, inv_ref, trail_ref,
    rows_buf, rows_all, inv3, py, pr, plft, w_out, wo, wm, wr, wl, kt, part, part_in,
    in_sem, rows_send, rows_recv, py_send, py_recv, pz_send, pz_recv,
    wo_send, wo_recv, wm_send, wm_recv, wz_send, wz_recv, pt_send, pt_recv,
):
    col = lax.axis_index("col")
    row = lax.axis_index("row")
    nz = n // 2
    z, y = col // 2, col % 2
    y_mate = z * 2 + 1 - y
    right, left = lax.rem(col + 2, n), lax.rem(col + n - 2, n)
    blk, width = x_ref.shape
    half = blk // 2
    quarter = blk // nr
    size = quarter // UNITS
    per = rows_ref.shape[0]

    barrier = pltpu.get_barrier_semaphore()

    def greet(**where):
        pl.semaphore_signal(barrier, inc=1, device_id=where, device_id_type=MESH)

    for d in range(1, n):
        greet(col=lax.rem(col + d, n))
    for d in range(1, nr):
        greet(row=lax.rem(row + d, nr))
        greet(row=lax.rem(row + d, nr), col=y_mate)
    loads = [
        pltpu.make_async_copy(src, dst, in_sem.at[i])
        for i, (src, dst) in enumerate(
            ((panel_hbm, panel), (x_hbm, x_ref), (inv_hbm, inv_ref), (trail_hbm, trail_ref))
        )
    ]
    for load in loads:
        load.start()
    rows_buf[col] = rows_ref[...].astype(F32)
    pl.semaphore_wait(barrier, n - 1 + 2 * (nr - 1))

    def remote(src, dst, send, recv, **where):
        return pltpu.make_async_remote_copy(
            src_ref=src, dst_ref=dst, send_sem=send, recv_sem=recv,
            device_id=where, device_id_type=MESH,
        )

    def rows_copy(d, slot):
        return remote(
            rows_buf.at[slot], rows_buf.at[slot], rows_send.at[d], rows_recv.at[slot],
            col=lax.rem(col + d, n),
        )

    for d in range(1, n):
        rows_copy(d, col).start()

    def unit(k):
        return pl.ds(pl.multiple_of(k * size, size), size)

    def own_unit(k):
        return pl.ds(pl.multiple_of(row * quarter + k * size, size), size)

    def py_copy(k):
        return remote(
            x_hbm.at[own_unit(k)], py.at[unit(k)], py_send.at[k], py_recv.at[k], col=y_mate
        )

    for k in range(UNITS):
        py_copy(k).start()
    for load in loads:
        load.wait()

    target = n // 4
    at = jnp.int32(0)
    for i in range(n):
        at = at + jnp.where(panel[i] == target, i, 0)
    root_here = at == col
    root_layer = at // 2 == z
    from_left = at // 2 <= z

    sums = jnp.zeros((blk, 128), F32)
    for j in range(0, width, 128):
        piece = x_ref[:, j:j + 128].astype(F32)
        sums = sums + piece * piece
    x_norm = jnp.sqrt(jnp.sum(sums.T, axis=0, keepdims=True) + EPS)
    x_inv = 1.0 / x_norm
    for i, term in enumerate(split3(inv_ref[...])):
        inv3[i] = term

    def block_kernel(a, a_f):
        a_norm = jnp.sqrt(jnp.sum(a_f * a_f, axis=1, keepdims=True) + EPS)
        u = dot_t(a, x_ref[...]) * (1.0 / a_norm) * x_inv
        return theta_of(u) * (a_norm * x_norm)

    def z_copy(buf, index, k, way, send, recv):
        return remote(
            buf.at[index], buf.at[index], send.at[way, k], recv.at[way, k],
            col=right if way == 0 else left,
        )

    def position(way):
        return z if way == 0 else nz - 1 - z

    def pass_on(buf, index, k, way, cand, send, recv):
        pos = position(way)

        @pl.when(pos == 0)
        def _():
            buf[index] = cand()

        @pl.when(pos > 0)
        def _():
            z_copy(buf, index, k, way, send, recv).wait_recv()
            buf[index] = lax.select(root_layer, cand(), buf[index])

        @pl.when(pos < nz - 1)
        def _():
            z_copy(buf, index, k, way, send, recv).start()

    def panel_slot(step):
        @pl.when(step < UNITS)
        def _():
            py_copy(step).wait_recv()
            own = x_ref[own_unit(step), :]
            py[unit(step), :] = lax.select(root_here, own, py[unit(step), :])

        for way, buf in enumerate((pr, plft)):
            k = step - HOP * position(way)

            @pl.when(jnp.logical_and(k >= 0, k < UNITS))
            def _():
                pass_on(buf, unit(k), k, way, lambda: py[unit(k), :], pz_send, pz_recv)

    def slots(first, last):
        @pl.loop(first, last)
        def _(step):
            panel_slot(step)

    def panel_group(g):
        sel = slice(g * quarter // GROUPS, (g + 1) * quarter // GROUPS)
        a = lax.select(from_left, pr[sel, :], plft[sel, :])
        kt[sel, :] = block_kernel(a, a.astype(F32))

    def work_rows():
        for d in range(1, n):
            slot = lax.rem(col + n - d, n)
            rows_copy(d, slot).wait_recv()
        for c in range(n):
            rows_all[c * per:(c + 1) * per, :] = rows_buf[c]
        a_f = rows_all[...]
        return block_kernel(a_f.astype(BF16), a_f)

    def wo_copy(d, slot):
        peer = lax.rem(row + d, nr)
        return remote(w_out.at[peer], wo.at[slot], wo_send.at[d], wo_recv.at[slot], row=peer)

    def wm_copy(d, slot):
        peer = lax.rem(row + d, nr)
        return remote(
            w_out.at[peer], wm.at[slot], wm_send.at[d], wm_recv.at[slot], row=peer, col=y_mate
        )

    def work_mid(a):
        low = product3(a[:, :half], [inv3[i, :half, :half] for i in range(3)], True)
        high = product3(a, [inv3[i, half:, :] for i in range(3)], True)
        return jnp.concatenate([low, high], axis=1)

    def work_w(mid):
        low = product3(mid, [inv3[i, :, :half] for i in range(3)], False)
        high = product3(mid[:, half:], [inv3[i, half:, half:] for i in range(3)], False)
        w = jnp.concatenate([low, high], axis=1)
        for j in range(nr):
            w_out[j] = w[:, j * quarter:(j + 1) * quarter]
        for d in range(nr):
            wm_copy(d, row).start()
        for d in range(1, nr):
            wo_copy(d, row).start()
        wo[row] = w_out[row]

    def work_exchange():
        for d in range(nr):
            slot = lax.rem(row + nr - d, nr)
            wm_copy(d, slot).wait_recv()
        for d in range(1, nr):
            slot = lax.rem(row + nr - d, nr)
            wo_copy(d, slot).wait_recv()
        for k in range(nr):
            wm[k] = lax.select(root_here, wo[k], wm[k])

    def w_hop(step):
        for way, buf in enumerate((wr, wl)):
            @pl.when(position(way) == step)
            def _():
                for k in range(nr):
                    pass_on(buf, k, k, way, lambda: wm[k], wz_send, wz_recv)

    last = UNITS + HOP * (nz - 1)
    first_group = last - UNITS + UNITS // GROUPS
    slots(0, 2)
    k_rows = work_rows()
    slots(2, 4)
    mid = work_mid(k_rows)
    slots(4, 6)
    work_w(mid)
    slots(6, first_group)
    work_exchange()
    w_hop(0)
    panel_group(0)
    for g in range(1, GROUPS):
        slots(first_group + (g - 1) * UNITS // GROUPS, first_group + g * UNITS // GROUPS)
        w_hop(g)
        panel_group(g)

    @pl.loop(GROUPS, nz)
    def _(step):
        w_hop(step)

    def part_copy(d, slot):
        peer = lax.rem(row + d, nr)
        return remote(part.at[peer], part_in.at[slot], pt_send.at[d], pt_recv.at[slot], row=peer)

    w = jnp.concatenate([lax.select(from_left, wr[j], wl[j]) for j in range(nr)], axis=0)
    update = jnp.dot(w, kt[...], precision=lax.Precision.HIGHEST, preferred_element_type=F32)
    group = update.shape[0] // nr
    for j in range(nr):
        part[j] = update[j * group:(j + 1) * group]
    for d in range(1, nr):
        part_copy(d, row).start()
    total = part[row]
    for d in range(1, nr):
        slot = lax.rem(row + nr - d, nr)
        part_copy(d, slot).wait_recv()
        total = total + part_in[slot]
    trail = trail_ref[...]
    out_ref[...] = lax.select(panel[col] > target, trail - total, trail)

    for d in range(1, n):
        rows_copy(d, col).wait_send()
    for k in range(UNITS):
        py_copy(k).wait_send()
    for d in range(nr):
        wm_copy(d, row).wait_send()
    for d in range(1, nr):
        wo_copy(d, row).wait_send()
        part_copy(d, row).wait_send()
    for way in (0, 1):
        @pl.when(position(way) < nz - 1)
        def _():
            for k in range(UNITS):
                z_copy((pr, plft)[way], unit(k), k, way, pz_send, pz_recv).wait_send()
            for k in range(nr):
                z_copy((wr, wl)[way], k, k, way, wz_send, wz_recv).wait_send()


def on_device(n, nr, panel, centres_cols, centres_rows, diag_inverse, trailing):
    blk, width = centres_cols.shape
    quarter = blk // nr
    per = centres_rows.shape[0]
    group = per * n
    dma = pltpu.SemaphoreType.DMA
    vmem = pl.BlockSpec(memory_space=pltpu.VMEM)
    hbm = pl.BlockSpec(memory_space=pltpu.HBM)
    return pl.pallas_call(
        functools.partial(kernel, n, nr),
        out_shape=jax.ShapeDtypeStruct(trailing.shape, F32),
        in_specs=[hbm, hbm, vmem, hbm, hbm],
        out_specs=vmem,
        scratch_shapes=[
            pltpu.SMEM(panel.shape, jnp.int32),
            pltpu.VMEM(centres_cols.shape, BF16),
            pltpu.VMEM(diag_inverse.shape, F32),
            pltpu.VMEM(trailing.shape, F32),
            pltpu.VMEM((n, per, width), F32),
            pltpu.VMEM((group, width), F32),
            pltpu.VMEM((3, blk, blk), BF16),
            pltpu.VMEM((quarter, width), BF16),
            pltpu.VMEM((quarter, width), BF16),
            pltpu.VMEM((quarter, width), BF16),
            pltpu.VMEM((nr, group, quarter), F32),
            pltpu.VMEM((nr, group, quarter), F32),
            pltpu.VMEM((nr, group, quarter), F32),
            pltpu.VMEM((nr, group, quarter), F32),
            pltpu.VMEM((nr, group, quarter), F32),
            pltpu.VMEM((quarter, blk), F32),
            pltpu.VMEM((nr, group, blk), F32),
            pltpu.VMEM((nr, group, blk), F32),
            dma((4,)),
            dma((n,)), dma((n,)),
            dma((UNITS,)), dma((UNITS,)),
            dma((2, UNITS)), dma((2, UNITS)),
            dma((nr,)), dma((nr,)),
            dma((nr,)), dma((nr,)),
            dma((2, nr)), dma((2, nr)),
            dma((nr,)), dma((nr,)),
        ],
        compiler_params=pltpu.CompilerParams(
            collective_id=0, has_side_effects=True, vmem_limit_bytes=48 * 2**20
        ),
    )(panel, centres_cols, centres_rows, diag_inverse, trailing)


def solution(mesh):
    return jax.shard_map(
        functools.partial(on_device, mesh.shape["col"], mesh.shape["row"]),
        mesh=mesh,
        in_specs=(P(), P("col", None), P(("row", "col"), None), P("col", None), P("row", "col")),
        out_specs=P("row", "col"),
        check_vma=False,
    )
```

time: 54 us -> 40.6 us (0.75)
  Pallas kernels: 48.5 us -> 35 us
    pallas_call x1, Pallas kernels: 48.5 us -> 35 us  [on_device(): pl.pallas_call(functools.partial(kernel, n, nr), out_shape=jax.ShapeDtype...]
where the time goes in v2:
time: 40.6 us; the launch traced here: 40.3 us
  Pallas kernels  35 us (86%)
  local copies, waits for them, and re-layouts  5.27 us (13%)
    pallas_call x1, Pallas kernels, on_device(): pl.pallas_call(functools.partial(kernel, n, nr), out_shape=jax.ShapeDtype...  35 us
    unnamed x11, local copies, waits for them, and re-layouts  5.27 us

profile of v2, /device:TPU:1, one launch (start us, length us, event | category | flops | bytes accessed | tf_op | source)
XLA Modules:
  0.0 40.3 jit_solution(2347187678185977877)
XLA Ops:
  0.0 0.0 copy-start
  0.0 1.2 %copy-done = bf16[512,1024]{1,0:T(8,128)(2,1)S(1)} copy-done((bf16[512,1024]{1,0:T(8,128)(2,1)S(1)}, bf16[512,1024]{1,0:T(8,128)(2,1)}, u32[]{:S(2)}) %copy-start) | copy-done | bytes 1048600
  1.2 0.0 copy-start.1
  1.2 1.2 %copy-done.1 = f32[512,512]{1,0:T(8,128)S(1)} copy-done((f32[512,512]{1,0:T(8,128)S(1)}, f32[512,512]{1,0:T(8,128)}, u32[]{:S(2)}) %copy-start.1) | copy-done | bytes 1048600
  2.5 0.0 copy-start.2
  2.5 0.8 %copy-done.2 = f32[32,512]{1,0:T(8,128)S(1)} copy-done((f32[32,512]{1,0:T(8,128)S(1)}, f32[32,512]{1,0:T(8,128)}, u32[]{:S(2)}) %copy-start.2) | copy-done | bytes 65560
  3.3 0.0 copy-start.3
  3.3 0.7 %copy-done.3 = bf16[4,1024]{1,0:T(4,128)(2,1)S(1)} copy-done((bf16[4,1024]{1,0:T(4,128)(2,1)S(1)}, bf16[4,1024]{1,0:T(4,128)(2,1)}, u32[]{:S(2)}) %copy-start.3) | copy-done | bytes 8216
  4.0 0.0 copy-start.4
  4.0 0.7 %copy-done.4 = s32[8]{0:T(128)S(1)} copy-done((s32[8]{0:T(128)S(1)}, s32[8]{0:T(128)}, u32[]{:S(2)}) %copy-start.4) | copy-done | bytes 56
  4.6 35.0 %shard_map.55 = f32[32,512]{1,0:T(8,128)S(1)} custom-call(s32[8]{0:T(128)S(1)} %copy-done.4, bf16[512,1024]{1,0:T(8,128)(2,1)S(1)} %copy-done, bf16[4,1024]{1,0:T(4,128)(2,1)S(1)} %copy-done.3, f32[512,512]{1,0:T(8,128)S(1)} %copy-done.1, f32[32,512]{1,0:T(8,128)S(1)} %copy-done.2), custom_call_target="tpu_custom_call" | custom-call | tf_op jit(solution)/shard_map/pallas_call | solution.py:341
  39.7 0.6 %copy.7 = f32[32,512]{1,0:T(8,128)} copy(f32[32,512]{1,0:T(8,128)S(1)} %shard_map.55) | data formatting | bytes 131072
Async XLA Ops:
  0.0 1.2 %copy-start = (bf16[512,1024]{1,0:T(8,128)(2,1)S(1)}, bf16[512,1024]{1,0:T(8,128)(2,1)}, u32[]{:S(2)}) copy-start(bf16[512,1024]{1,0:T(8,128)(2,1)} %x_hbm.1) | copy-start | bytes 3145732
  1.2 1.2 %copy-start.1 = (f32[512,512]{1,0:T(8,128)S(1)}, f32[512,512]{1,0:T(8,128)}, u32[]{:S(2)}) copy-start(f32[512,512]{1,0:T(8,128)} %inv_hbm.1) | copy-start | bytes 3145732
  2.5 0.8 %copy-start.2 = (f32[32,512]{1,0:T(8,128)S(1)}, f32[32,512]{1,0:T(8,128)}, u32[]{:S(2)}) copy-start(f32[32,512]{1,0:T(8,128)} %trail_hbm.1) | copy-start | bytes 196612
  3.3 0.7 %copy-start.3 = (bf16[4,1024]{1,0:T(4,128)(2,1)S(1)}, bf16[4,1024]{1,0:T(4,128)(2,1)}, u32[]{:S(2)}) copy-start(bf16[4,1024]{1,0:T(4,128)(2,1)} %rows_ref.1) | copy-start | bytes 24580
  4.0 0.7 %copy-start.4 = (s32[8]{0:T(128)S(1)}, s32[8]{0:T(128)}, u32[]{:S(2)}) copy-start(s32[8]{0:T(128)} %panel_hbm.1) | copy-start | bytes 100
